TPU v7x, 32 devices: a whole 2x2x4 slice. The times are simulated.
32 devices in a mesh: dp: 8 (over z, x), expert: 4 (over y, core).
Axes of the slice: x: 2, y: 2, z: 4, core: 2. Of those that a mesh axis runs over, the one named last changes fastest.
Arguments:
- tokens: bfloat16 [192, 6144], P('expert', 'dp'), may hold values from -6 to 6
- routing: int32 [192, 2], P('expert'), may hold values from 0 to 3, all different within a row; in each aligned block of 48 rows (0 to 47, 48 to 95, ...) at most 36 rows name the same one
- gates: int32 [192, 2], P('expert'), may hold values from 1 to 255
- w_gate: bfloat16 [4, 8192, 6144], P('expert', 'dp'), may hold values from -0.109375 to 0.109375
- w_up: bfloat16 [4, 8192, 6144], P('expert', 'dp'), may hold values from -0.078125 to 0.078125
- w_down: bfloat16 [4, 8192, 6144], P('expert', 'dp'), may hold values from -0.09375 to 0.09375
- cotangent: bfloat16 [192, 6144], P('expert', 'dp'), may hold values from -6 to 6
Outputs:
- mixed: bfloat16 [192, 6144], P('expert', 'dp')
- token_grad: bfloat16 [192, 6144], P('expert', 'dp')
- down_grad: bfloat16 [4, 8192, 6144], P('expert', 'dp')
Inputs may be any that keep to these rules, and one draw needn't show every extreme that they name: `routing`: A token's two experts differ; in each aligned block of 48 tokens no expert is named by more than 36 choices, a bound that some block reaches.
All inputs are finite; a program needn't handle non-finite values.
Results may differ from a plain program's by a relative error of at most 0.0065.
Values may be sent and summed in bfloat16 or wider, within the bound.
A program may use at most 128 MiB of HBM per device.

v0:
```python
import jax
import jax.numpy as jnp
from jax import lax
from jax.sharding import PartitionSpec as P


def slot_tables(routing, gates, experts, capacity):
    pair_ids = routing.reshape(-1)
    expert_ids = lax.iota(jnp.int32, experts)
    onehot = (pair_ids[:, None] == expert_ids[None, :]).astype(jnp.int32)
    earlier = jnp.cumsum(onehot, axis=0) - onehot
    slot_rank = jnp.sum(earlier * onehot, axis=1)
    targets = (pair_ids * capacity + slot_rank).reshape(routing.shape)
    slot_ids = lax.iota(jnp.int32, experts * capacity)
    matches = slot_ids[:, None, None] == targets[None, :, :]
    placing = jnp.sum(matches.astype(jnp.float32), axis=2)
    weighting = jnp.sum(
        jnp.where(matches, gates[None, :, :].astype(jnp.float32) / 256.0, 0.0), axis=2
    )
    return (placing.astype(jnp.bfloat16), weighting.astype(jnp.bfloat16))


def per_device(tokens, routing, gates, w_gate, w_up, w_down, cotangent):
    experts = lax.axis_size("expert")
    capacity = 3 * tokens.shape[0] // experts
    placing, weighting = slot_tables(routing, gates, experts, capacity)
    gate_mat = w_gate[0]
    up_mat = w_up[0]
    down_mat = w_down[0]
    send_rows = jnp.dot(placing, tokens, preferred_element_type=jnp.float32).astype(jnp.bfloat16)
    send_grads = jnp.dot(weighting, cotangent, preferred_element_type=jnp.float32).astype(
        jnp.bfloat16
    )
    send_rows = send_rows.reshape(experts, capacity, -1)
    send_grads = send_grads.reshape(experts, capacity, -1)
    part_rows, part_grads = (
        lax.all_to_all(send_rows, "expert", split_axis=0, concat_axis=0, tiled=True),
        lax.all_to_all(send_grads, "expert", split_axis=0, concat_axis=0, tiled=True),
    )
    rows_in, grads_in = (
        lax.all_gather(part_rows, "dp", axis=2, tiled=True),
        lax.all_gather(part_grads, "dp", axis=2, tiled=True),
    )
    width = rows_in.shape[2]
    rows_in = rows_in.reshape(-1, width)
    grads_in = grads_in.reshape(-1, width)
    row_count = rows_in.shape[0]
    dims = (((1,), (1,)), ((), ()))
    across = (((0,), (1,)), ((), ()))
    pre_gate = lax.dot_general(rows_in, gate_mat, dims, preferred_element_type=jnp.float32)
    pre_up = lax.dot_general(rows_in, up_mat, dims, preferred_element_type=jnp.float32)
    sigmoid_gate = jax.nn.sigmoid(pre_gate)
    swish = pre_gate * sigmoid_gate
    hidden = (swish * pre_up).astype(jnp.bfloat16)
    hidden_grad = lax.dot_general(grads_in, down_mat, dims, preferred_element_type=jnp.float32)
    gate_grad = (
        hidden_grad * pre_up * sigmoid_gate * (1.0 + pre_gate * (1.0 - sigmoid_gate))
    ).astype(jnp.bfloat16)
    up_grad = (hidden_grad * swish).astype(jnp.bfloat16)
    down_grad = lax.dot_general(
        hidden, grads_in, (((0,), (0,)), ((), ())), preferred_element_type=jnp.float32
    )
    down_grad = down_grad.astype(jnp.bfloat16)[None]
    inward = lax.dot_general(gate_mat, gate_grad, across, preferred_element_type=jnp.float32)
    summed = lax.psum_scatter(
        jnp.concatenate(
            [
                lax.dot_general(down_mat, hidden, across, preferred_element_type=jnp.float32),
                inward
                + lax.dot_general(up_mat, up_grad, across, preferred_element_type=jnp.float32),
            ],
            axis=1,
        ),
        "dp",
        scatter_dimension=0,
        tiled=True,
    )
    out_summed = summed[:, :row_count]
    in_summed = summed[:, row_count:]
    expert_out = out_summed.T.astype(jnp.bfloat16).reshape(experts, capacity, -1)
    expert_back = in_summed.T.astype(jnp.bfloat16).reshape(experts, capacity, -1)
    back_out, back_grad = (
        lax.all_to_all(expert_out, "expert", split_axis=0, concat_axis=0, tiled=True),
        lax.all_to_all(expert_back, "expert", split_axis=0, concat_axis=0, tiled=True),
    )
    back_out = back_out.reshape(experts * capacity, -1)
    back_grad = back_grad.reshape(experts * capacity, -1)
    collect = (((0,), (0,)), ((), ()))
    mixed = lax.dot_general(
        weighting, back_out, collect, preferred_element_type=jnp.float32
    ).astype(jnp.bfloat16)
    token_grad = lax.dot_general(
        placing, back_grad, collect, preferred_element_type=jnp.float32
    ).astype(jnp.bfloat16)
    return (mixed, token_grad, down_grad)


def solution(mesh):
    return jax.shard_map(
        per_device,
        mesh=mesh,
        in_specs=(
            P("expert", "dp"),
            P("expert", None),
            P("expert", None),
            P("expert", "dp", None),
            P("expert", "dp", None),
            P("expert", "dp", None),
            P("expert", "dp"),
        ),
        out_specs=(P("expert", "dp"), P("expert", "dp"), P("expert", "dp", None)),
        check_vma=False,
    )
```

profile of v0, /device:TPU:0, one launch (start us, length us, event | category | flops | bytes accessed | tf_op | source)
XLA Modules:
  0.0 306.0 jit_solution(14273849108212105506)
XLA Ops:
  7.2 0.0 copy-start
  7.2 0.0 all-gather.3.cloned.1.call-start
  7.2 0.7 convert_multiply_fusion
  7.9 0.8 copy.22
  8.7 0.1 eq.29
  8.8 0.1 fusion.24
  8.9 0.1 reduce_window_sum.11
  9.0 0.2 select_reduce_fusion.1
  9.2 0.1 reduce_sum.30
  9.3 0.1 copy.23
  9.4 0.7 multiply_add_fusion
  10.1 0.1 convert_reduce_fusion
  10.2 0.2 convolution_convert_fusion.1
  10.5 10.0 %all_to_all.20 = bf16[4,36,768]{2,1,0:T(8,128)(2,1)} all-to-all(bf16[4,36,768]{2,1,0:T(8,128)(2,1)S(1)} %reshape.41), channel_id=1, replica_groups=mesh['dp'=8,'expert'=4] {'expert'}, dimensions={0} | all-to-all | bytes 442368 | tf_op jit(solution)/shard_map/all_to_all | solution.py:37
  20.5 0.0 all-gather.3.cloned.1.call-update
  20.6 0.0 all-gather.5.cloned.1.call-start
  20.6 1.1 convolution_convert_fusion
  21.8 8.9 %all_to_all.21 = bf16[4,36,768]{2,1,0:T(8,128)(2,1)} all-to-all(bf16[4,36,768]{2,1,0:T(8,128)(2,1)S(1)} %reshape.43), channel_id=1, replica_groups=mesh['dp'=8,'expert'=4] {'expert'}, dimensions={0} | all-to-all | bytes 442368 | tf_op jit(solution)/shard_map/all_to_all | solution.py:38
  30.7 0.0 all-gather.5.cloned.1.call-update
  30.7 0.0 reduce-scatter.2.cloned.1.call-start
  30.8 39.0 %all-gather.3.cloned.1.call-done = bf16[4,36,6144]{2,1,0:T(8,128)(2,1)} async-done(((bf16[4,36,768]{2,1,0:T(8,128)(2,1)}), bf16[4,36,6144]{2,1,0:T(8,128)(2,1)}) %all-gather.3.cloned.1.call-update) | async-done | bytes 1769488 | tf_op jit(solution)/shard_map/all_gather | solution.py:41
  69.8 1.7 reshape.42
  71.5 0.0 copy-start.2
  71.5 9.8 %fusion.10 = f32[144,1024]{1,0:T(8,128)} fusion(bf16[144,6144]{1,0:T(8,128)(2,1)S(1)} %reshape.42, bf16[1,1024,6144]{2,1,0:T(8,128)(2,1)} %param.10), kind=kOutput, calls=%fused_computation.10 | convolution fusion | flops 1811939328 | bytes 14942208 | tf_op jit(solution)/shard_map/dot_general | solution.py:50
  81.3 6.3 %multiply_convert_fusion.2 = (bf16[144,1024]{1,0:T(8,128)(2,1)}, f32[144,1024]{1,0:T(8,128)}) fusion(f32[144,1024]{1,0:T(8,128)} %fusion.10, bf16[144,6144]{1,0:T(8,128)(2,1)S(1)} %reshape.42, bf16[1,1024,6144]{2,1,0:T(8,128)(2,1)S(1)} %copy-done.2), kind=kOutput, calls=%fused_computation.23 | convolution fusion | flops 1812824064 | bytes 15826944 | tf_op jit(solution)/shard_map/dot_general | solution.py:51
  87.6 31.2 %all-gather.5.cloned.1.call-done = bf16[4,36,6144]{2,1,0:T(8,128)(2,1)} async-done(((bf16[4,36,768]{2,1,0:T(8,128)(2,1)}), bf16[4,36,6144]{2,1,0:T(8,128)(2,1)}) %all-gather.5.cloned.1.call-update) | async-done | bytes 1769488 | tf_op jit(solution)/shard_map/all_gather | solution.py:42
  118.8 1.9 reshape.44
  120.7 0.0 copy-start.3
  120.7 0.0 slice-start
  120.7 0.0 slice-start.1
  120.7 9.0 %fusion = f32[144,1024]{1,0:T(8,128)S(1)} fusion(bf16[144,6144]{1,0:T(8,128)(2,1)S(1)} %reshape.44, bf16[1,1024,6144]{2,1,0:T(8,128)(2,1)} %param.12), kind=kOutput, calls=%fused_computation | convolution fusion | flops 1811939328 | bytes 14942208 | tf_op jit(solution)/shard_map/dot_general | solution.py:55
  129.8 0.0 slice-start.2
  129.8 6.8 %fusion.4 = f32[144,6144]{1,0:T(8,128)S(1)} fusion(bf16[1,1024,6144]{2,1,0:T(8,128)(2,1)} %param.11, f32[144,1024]{1,0:T(8,128)S(1)} %fusion, f32[144,1024]{1,0:T(8,128)S(1)} %copy-done.3), kind=kOutput, calls=%fused_computation.4 | convolution fusion | flops 1812824064 | bytes 17301504 | tf_op jit(solution)/shard_map/dot_general | solution.py:70
  136.7 2.1 fusion.12
  138.7 6.8 %fusion.18 = f32[6144,144]{0,1:T(8,128)S(1)} fusion(f32[144,6144]{1,0:T(8,128)S(1)} %fusion.4, bf16[1,1024,6144]{2,1,0:T(8,128)(2,1)} %param.10, f32[144,1024]{1,0:T(8,128)S(1)} %copy-done.3, f32[144,1024]{1,0:T(8,128)S(1)} %fusion, f32[144,1024]{1,0:T(8,128)S(1)} %copy-done.4), kind=kOutput, calls=%fused_computation.15 | convolution fusion | flops 1814298624 | bytes 21430272 | tf_op jit(solution)/shard_map/dot_general | solution.py:64
  145.5 3.5 %pad_maximum_fusion = f32[6144,288]{0,1:T(8,128)} fusion(f32[6144,144]{0,1:T(8,128)S(1)} %fusion.18, f32[6144,144]{0,1:T(8,128)S(1)} %fusion.12), kind=kLoop, calls=%fused_computation.16 | loop fusion | flops 1769472 | bytes 14155776 | tf_op jit(solution)/shard_map/concatenate | solution.py:66
  149.0 0.0 reduce-scatter.2.cloned.1.call-update
  149.1 127.6 %reduce-scatter.2.cloned.1.call-done = f32[768,288]{0,1:T(8,128)} async-done(((f32[6144,288]{0,1:T(8,128)}), f32[768,288]{0,1:T(8,128)}) %reduce-scatter.2.cloned.1.call-update) | async-done | bytes 884752 | tf_op jit(solution)/shard_map/reduce_scatter | solution.py:65
  276.6 1.2 convert.4
  277.9 0.7 reshape.47
  278.6 3.4 %all-to-all-start.3 = ((bf16[4,36,768]{2,1,0:T(8,128)(2,1)}), bf16[4,36,768]{2,1,0:T(8,128)(2,1)S(1)}, u32[]{:S(2)}, u32[]{:S(2)}) async-start(bf16[4,36,768]{2,1,0:T(8,128)(2,1)} %reshape.47), calls=%async_computation.4 | async-start | bytes 491520 | tf_op jit(solution)/shard_map/all_to_all | solution.py:84
  282.0 0.0 copy-start.1
  282.0 6.7 %convert_bitcast_fusion = bf16[1,1024,6144]{2,1,0:T(8,128)(2,1)} fusion(bf16[144,1024]{1,0:T(8,128)(2,1)S(1)} %copy-done.5, bf16[144,6144]{1,0:T(8,128)(2,1)S(1)} %reshape.44), kind=kOutput, calls=%fused_computation.12 | convolution fusion | flops 1818230784 | bytes 14647296 | tf_op jit(solution)/shard_map/dot_general | solution.py:60
  288.7 0.7 reshape.45
  289.4 3.4 %all-to-all-start.2 = ((bf16[4,36,768]{2,1,0:T(8,128)(2,1)}), bf16[4,36,768]{2,1,0:T(8,128)(2,1)S(1)}, u32[]{:S(2)}, u32[]{:S(2)}) async-start(bf16[4,36,768]{2,1,0:T(8,128)(2,1)} %reshape.45), calls=%async_computation.3 | async-start | bytes 491520 | tf_op jit(solution)/shard_map/all_to_all | solution.py:83
  292.9 0.8 convolution_convert_fusion.2
  293.7 5.0 %all-to-all-done.2 = bf16[4,36,768]{2,1,0:T(8,128)(2,1)S(1)} async-done(((bf16[4,36,768]{2,1,0:T(8,128)(2,1)}), bf16[4,36,768]{2,1,0:T(8,128)(2,1)S(1)}, u32[]{:S(2)}, u32[]{:S(2)}) %all-to-all-start.2) | async-done | bytes 221216 | tf_op jit(solution)/shard_map/all_to_all | solution.py:83
  298.7 0.8 convolution_convert_fusion.3
  (18 shorter events, 0.2 us)
Async XLA Ops:
  7.2 3.0 copy-start
  7.2 62.6 %all-gather.3.cloned.1.call-start = ((), (), s32[]{:S(2)}) async-start(), calls=%async_computation.5 | async-start | bytes 2211840 | tf_op jit(solution)/shard_map/all_gather | solution.py:41
  20.6 98.3 %all-gather.5.cloned.1.call-start = ((), (), s32[]{:S(2)}) async-start(), calls=%async_computation.6 | async-start | bytes 2211840 | tf_op jit(solution)/shard_map/all_gather | solution.py:42
  30.7 245.9 %reduce-scatter.2.cloned.1.call-start = ((), (), s32[]{:S(2)}) async-start(), calls=%async_computation.7 | async-start | bytes 7962624 | tf_op jit(solution)/shard_map/reduce_scatter | solution.py:65
  71.5 9.8 %copy-start.2 = (bf16[1,1024,6144]{2,1,0:T(8,128)(2,1)S(1)}, bf16[1,1024,6144]{2,1,0:T(8,128)(2,1)}, u32[]{:S(2)}) copy-start(bf16[1,1024,6144]{2,1,0:T(8,128)(2,1)} %param.11) | copy-start | bytes 37748740
  120.7 9.1 %copy-start.3 = (f32[144,1024]{1,0:T(8,128)S(1)}, f32[144,1024]{1,0:T(8,128)}, u32[]{:S(2)}) copy-start(f32[144,1024]{1,0:T(8,128)} %fusion.10) | copy-start | bytes 1769476
  120.7 15.9 %slice-start = ((s8[12582912]{0:T(1024)(128)(4,1)}), s8[4194304]{0:T(1024)(128)(4,1)S(1)}, s32[]{:S(2)}) async-start(s8[12582912]{0:T(1024)(128)(4,1)} %bitcast.47), calls=%async_computation.8 | async-start | bytes 8388608
  120.7 15.9 %slice-start.1 = ((s8[12582912]{0:T(1024)(128)(4,1)}), s8[4194304]{0:T(1024)(128)(4,1)S(1)}, s32[]{:S(2)}) async-start(s8[12582912]{0:T(1024)(128)(4,1)} %bitcast.47), calls=%async_computation.9 | async-start | bytes 8388608
  129.8 6.9 %slice-start.2 = ((s8[12582912]{0:T(1024)(128)(4,1)}), s8[4194304]{0:T(1024)(128)(4,1)S(1)}, s32[]{:S(2)}) async-start(s8[12582912]{0:T(1024)(128)(4,1)} %bitcast.47), calls=%async_computation.10 | async-start | bytes 8388608
  129.8 6.9 %copy-start.5 = (bf16[144,1024]{1,0:T(8,128)(2,1)S(1)}, bf16[144,1024]{1,0:T(8,128)(2,1)}, u32[]{:S(2)}) copy-start(bf16[144,1024]{1,0:T(8,128)(2,1)} %get-tuple-element.7) | copy-start | bytes 884740
  136.7 2.1 copy-start.4
  278.6 10.8 %all-to-all-start.3 = ((bf16[4,36,768]{2,1,0:T(8,128)(2,1)}), bf16[4,36,768]{2,1,0:T(8,128)(2,1)S(1)}, u32[]{:S(2)}, u32[]{:S(2)}) async-start(bf16[4,36,768]{2,1,0:T(8,128)(2,1)} %reshape.47), calls=%async_computation.4 | async-start | bytes 491520 | tf_op jit(solution)/shard_map/all_to_all | solution.py:84
  282.0 17.5 %copy-start.1 = (bf16[48,768]{1,0:T(8,128)(2,1)S(1)}, bf16[48,768]{1,0:T(8,128)(2,1)}, u32[]{:S(2)}) copy-start(bf16[48,768]{1,0:T(8,128)(2,1)} %param.7) | copy-start | bytes 221188
  289.4 9.2 %all-to-all-start.2 = ((bf16[4,36,768]{2,1,0:T(8,128)(2,1)}), bf16[4,36,768]{2,1,0:T(8,128)(2,1)S(1)}, u32[]{:S(2)}, u32[]{:S(2)}) async-start(bf16[4,36,768]{2,1,0:T(8,128)(2,1)} %reshape.45), calls=%async_computation.3 | async-start | bytes 491520 | tf_op jit(solution)/shard_map/all_to_all | solution.py:83
Sparse Core Ops, SparseCore 0:
  20.7 49.0 all-gather.2
  71.9 46.8 all-gather.4
  149.2 127.3 reduce-scatter.1
where the time goes:
time: 307 us; the launch traced here: 306 us
  waiting for transfers between devices  203 us (66%)
  matrix products  50.4 us (16%)
  blocking collectives  18.9 us (6%)
  between operations  14 us (5%)
  starting transfers between devices  6.91 us (2%)
  other arithmetic  6.57 us (2%)
  local copies, waits for them, and re-layouts  6.43 us (2%)
    reduce_scatter x1, waiting for transfers between devices, per_device(): lax.psum_scatter(jnp.concatenate([lax.dot_general(down_mat, hidden, acros...  128 us
    all_gather x1, waiting for transfers between devices, per_device(): lax.all_gather(part_rows, 'dp', axis=2, tiled=True)  39 us
    all_gather x1, waiting for transfers between devices, per_device(): lax.all_gather(part_grads, 'dp', axis=2, tiled=True)  31.2 us
    all_to_all x1, blocking collectives, per_device(): lax.all_to_all(send_rows, 'expert', split_axis=0, concat_axis=0, tiled=True)  10 us
    dot_general x1, matrix products, per_device(): lax.dot_general(rows_in, gate_mat, dims, preferred_element_type=jnp.float32)  9.83 us
    dot_general x1, matrix products, per_device(): lax.dot_general(grads_in, down_mat, dims, preferred_element_type=jnp.floa...  9.02 us
    all_to_all x1, blocking collectives, per_device(): lax.all_to_all(send_grads, 'expert', split_axis=0, concat_axis=0, tiled=T...  8.92 us
    dot_general x1, matrix products, per_device(): lax.dot_general(up_mat, up_grad, across, preferred_element_type=jnp.float32)  6.8 us
  transfers between devices with their start and end apart: 5, of which 4 were waited for; matrix products, arithmetic and copies ran while one was open for 9% of the time, Pallas kernels for 0%

commit v1 on v0

--- a/solution.py
+++ b/solution.py
@@ -1,5 +1,7 @@
 import jax
 import jax.numpy as jnp
+import jax.experimental.pallas as pl
+from jax.experimental.pallas import tpu as pltpu
 from jax import lax
 from jax.sharding import PartitionSpec as P
 
@@ -95,9 +97,297 @@
     return (mixed, token_grad, down_grad)
 
 
+MESH = pl.DeviceIdType.MESH
+PARTS = 3
+ORDERS = (
+    ("zh", "zl", "x", "y", "core"),
+    ("zh", "y", "zl", "x", "core"),
+    ("zh", "x", "y", "zl", "core"),
+)
+STEPS = 5
+
+
+def own_bits():
+    dp, expert = lax.axis_index("dp"), lax.axis_index("expert")
+    own = {
+        "zh": dp // 4,
+        "zl": (dp // 2) % 2,
+        "x": dp % 2,
+        "y": expert // 2,
+        "core": expert % 2,
+    }
+    return {name: (bit, 1 - bit) for name, bit in own.items()}
+
+
+def place(bits, flipped):
+    at = {name: pair[1 if name in flipped else 0] for name, pair in bits.items()}
+    return at["zh"] * 4 + at["zl"] * 2 + at["x"], at["y"] * 2 + at["core"]
+
+
+def partner(bits, name):
+    dp, expert = place(bits, (name,))
+    return {"dp": dp, "expert": expert}
+
+
+def flips(order, slot):
+    return tuple(order[step] for step in range(STEPS) if slot >> step & 1)
+
+
+def greet(others):
+    barrier = pltpu.get_barrier_semaphore()
+    for other in others:
+        pl.semaphore_signal(barrier, inc=1, device_id=other, device_id_type=MESH)
+    pl.semaphore_wait(barrier, len(others))
+
+
+def gather_kernel(mine, meta, out, metas, slots, sends, recvs, meta_sends, meta_recvs):
+    rows, width = mine.shape
+    part_rows = rows // PARTS
+    bits = own_bits()
+    dp, expert = place(bits, ())
+    row_of = [(("core",)), (("y",)), ("y", "core")]
+    peers = []
+    for names in row_of:
+        peers.append({"dp": dp, "expert": place(bits, names)[1]})
+    others = [partner(bits, name) for name in ("zh", "zl", "x", "y", "core")] + [peers[2]]
+    greet(others)
+
+    def copy(part, step):
+        count = 1 << step
+        return pltpu.make_async_remote_copy(
+            src_ref=slots.at[part, pl.ds(0, count)],
+            dst_ref=slots.at[part, pl.ds(count, count)],
+            send_sem=sends.at[part, step],
+            recv_sem=recvs.at[part, step],
+            device_id=partner(bits, ORDERS[part][step]),
+            device_id_type=MESH,
+        )
+
+    def settle(part, first, count):
+        for slot in range(first, first + count):
+            at_dp, at_expert = place(bits, flips(ORDERS[part], slot))
+            row = pl.multiple_of(at_expert * rows + part * part_rows, 16)
+            column = pl.multiple_of(at_dp * width, 128)
+            out[pl.ds(row, part_rows), pl.ds(column, width)] = slots[part, slot]
+
+    for part in range(PARTS):
+        slots[part, 0] = mine[part * part_rows:(part + 1) * part_rows, :]
+        copy(part, 0).start()
+    meta_copies = []
+    for i, peer in enumerate(peers):
+        meta_copies.append(
+            pltpu.make_async_remote_copy(
+                src_ref=meta,
+                dst_ref=metas.at[i + 1],
+                send_sem=meta_sends.at[i],
+                recv_sem=meta_recvs.at[i],
+                device_id=peer,
+                device_id_type=MESH,
+            )
+        )
+        meta_copies[-1].start()
+    metas[0] = meta[...]
+    for part in range(PARTS):
+        settle(part, 0, 1)
+    for step in range(STEPS):
+        for part in range(PARTS):
+            copy(part, step).wait_recv()
+            if step + 1 < STEPS:
+                copy(part, step + 1).start()
+            else:
+                settle(part, 1 << step, 1 << step)
+        if step + 1 < STEPS:
+            for part in range(PARTS):
+                settle(part, 1 << step, 1 << step)
+    for each in meta_copies:
+        each.wait()
+    for step in range(STEPS):
+        for part in range(PARTS):
+            copy(part, step).wait_send()
+
+
+def scatter_kernel(partial, out, slots, inbox, sends, recvs):
+    rows, width = out.shape
+    part_rows = rows // PARTS
+    bits = own_bits()
+    greet([partner(bits, name) for name in ("zh", "zl", "x", "y", "core")])
+
+    def copy(part, step):
+        count = 1 << step
+        return pltpu.make_async_remote_copy(
+            src_ref=slots.at[part, pl.ds(count, count)],
+            dst_ref=inbox.at[part, pl.ds(count, count)],
+            send_sem=sends.at[part, step],
+            recv_sem=recvs.at[part, step],
+            device_id=partner(bits, ORDERS[part][step]),
+            device_id_type=MESH,
+        )
+
+    def pick(part, first, count):
+        for slot in range(first, first + count):
+            at_dp, at_expert = place(bits, flips(ORDERS[part], slot))
+            row = pl.multiple_of(at_expert * rows + part * part_rows, 16)
+            column = pl.multiple_of(at_dp * width, 128)
+            slots[part, slot] = partial[pl.ds(row, part_rows), pl.ds(column, width)]
+
+    def add(part, step, first, count):
+        for slot in range(first, first + count):
+            total = slots[part, slot].astype(jnp.float32) + inbox[
+                part, (1 << step) + slot
+            ].astype(jnp.float32)
+            slots[part, slot] = total.astype(jnp.bfloat16)
+
+    top = STEPS - 1
+    for part in range(PARTS):
+        pick(part, 1 << top, 1 << top)
+        copy(part, top).start()
+    for part in range(PARTS):
+        pick(part, 0, 1 << top)
+    for step in range(top, 0, -1):
+        half = 1 << (step - 1)
+        for part in range(PARTS):
+            copy(part, step).wait_recv()
+            add(part, step, half, half)
+            copy(part, step - 1).start()
+        for part in range(PARTS):
+            add(part, step, 0, half)
+    for part in range(PARTS):
+        copy(part, 0).wait_recv()
+        total = slots[part, 0].astype(jnp.float32) + inbox[part, 1].astype(jnp.float32)
+        out[part * part_rows:(part + 1) * part_rows, :] = total.astype(jnp.bfloat16)
+    for step in range(STEPS):
+        for part in range(PARTS):
+            copy(part, step).wait_send()
+
+
+def vmem():
+    return pl.BlockSpec(memory_space=pltpu.VMEM)
+
+
+def gather_all(mine, meta):
+    rows, width = mine.shape
+    part_rows = rows // PARTS
+    dma = pltpu.SemaphoreType.DMA
+    return pl.pallas_call(
+        gather_kernel,
+        out_shape=(
+            jax.ShapeDtypeStruct((4 * rows, 8 * width), jnp.bfloat16),
+            jax.ShapeDtypeStruct((4,) + meta.shape, jnp.bfloat16),
+        ),
+        in_specs=[vmem(), vmem()],
+        out_specs=(vmem(), vmem()),
+        scratch_shapes=[
+            pltpu.VMEM((PARTS, 1 << STEPS, part_rows, width), jnp.bfloat16),
+            dma((PARTS, STEPS)),
+            dma((PARTS, STEPS)),
+            dma((3,)),
+            dma((3,)),
+        ],
+        compiler_params=pltpu.CompilerParams(
+            collective_id=0, has_side_effects=True, vmem_limit_bytes=32 << 20
+        ),
+    )(mine, meta)
+
+
+def scatter_sum(partial, rows, width):
+    part_rows = rows // PARTS
+    dma = pltpu.SemaphoreType.DMA
+    return pl.pallas_call(
+        scatter_kernel,
+        out_shape=jax.ShapeDtypeStruct((rows, width), jnp.bfloat16),
+        in_specs=[vmem()],
+        out_specs=vmem(),
+        scratch_shapes=[
+            pltpu.VMEM((PARTS, 1 << STEPS, part_rows, width), jnp.bfloat16),
+            pltpu.VMEM((PARTS, 1 << STEPS, part_rows, width), jnp.bfloat16),
+            dma((PARTS, STEPS)),
+            dma((PARTS, STEPS)),
+        ],
+        compiler_params=pltpu.CompilerParams(
+            collective_id=1, has_side_effects=True, vmem_limit_bytes=32 << 20
+        ),
+    )(partial)
+
+
+def per_device_cube(tokens, routing, gates, w_gate, w_up, w_down, cotangent):
+    experts = lax.axis_size("expert")
+    own = lax.axis_index("expert")
+    count, width = tokens.shape
+    capacity = 3 * count // experts
+    row_count = experts * capacity
+    gate_mat, up_mat, down_mat = w_gate[0], w_up[0], w_down[0]
+    meta = jnp.concatenate([routing.T, gates.T], axis=0).astype(jnp.bfloat16)
+    meta = jnp.pad(meta, ((0, 12), (0, 128 - count)))
+    everything, metas = gather_all(jnp.concatenate([tokens, cotangent], axis=0), meta)
+    block = lax.iota(jnp.int32, experts)
+    metas = jnp.take(metas, block ^ own, axis=0)[:, :4, :count].astype(jnp.float32)
+    named = metas[:, :2] == own.astype(jnp.float32)
+    hit = jnp.sum(named.astype(jnp.float32), axis=1)
+    weight = jnp.sum(jnp.where(named, metas[:, 2:], 0.0), axis=1) / 256.0
+    place_id = lax.iota(jnp.int32, count)
+    before = (place_id[:, None] < place_id[None, :]).astype(jnp.bfloat16)
+    rank = jnp.dot(hit.astype(jnp.bfloat16), before, preferred_element_type=jnp.float32)
+    target = rank.astype(jnp.int32) + block[:, None] * capacity
+    matches = (lax.iota(jnp.int32, row_count)[:, None, None] == target[None]) & (hit > 0.5)[None]
+    placing = matches.astype(jnp.bfloat16)
+    weighting = jnp.where(matches, weight[None], 0.0).astype(jnp.bfloat16)
+    none = jnp.zeros_like(placing)
+
+    def joined(first, second):
+        upper = jnp.concatenate([first, none], axis=2).reshape(row_count, -1)
+        lower = jnp.concatenate([none, second], axis=2).reshape(row_count, -1)
+        return jnp.concatenate([upper, lower], axis=0)
+
+    into, back = joined(placing, weighting), joined(weighting, placing)
+    both = jnp.dot(into, everything, preferred_element_type=jnp.float32).astype(jnp.bfloat16)
+    rows_in, grads_in = both[:row_count], both[row_count:]
+    dims = (((1,), (1,)), ((), ()))
+    across = (((0,), (1,)), ((), ()))
+    pre_gate = lax.dot_general(rows_in, gate_mat, dims, preferred_element_type=jnp.float32)
+    pre_up = lax.dot_general(rows_in, up_mat, dims, preferred_element_type=jnp.float32)
+    sigmoid_gate = jax.nn.sigmoid(pre_gate)
+    swish = pre_gate * sigmoid_gate
+    hidden = (swish * pre_up).astype(jnp.bfloat16)
+    hidden_grad = lax.dot_general(grads_in, down_mat, dims, preferred_element_type=jnp.float32)
+    gate_grad = (
+        hidden_grad * pre_up * sigmoid_gate * (1.0 + pre_gate * (1.0 - sigmoid_gate))
+    ).astype(jnp.bfloat16)
+    up_grad = (hidden_grad * swish).astype(jnp.bfloat16)
+    down_grad = lax.dot_general(
+        hidden, grads_in, (((0,), (0,)), ((), ())), preferred_element_type=jnp.float32
+    )
+    down_grad = down_grad.astype(jnp.bfloat16)[None]
+    outward = lax.dot_general(down_mat, hidden, across, preferred_element_type=jnp.float32)
+    inward = lax.dot_general(
+        gate_mat, gate_grad, across, preferred_element_type=jnp.float32
+    ) + lax.dot_general(up_mat, up_grad, across, preferred_element_type=jnp.float32)
+    sums = jnp.concatenate(
+        [outward.astype(jnp.bfloat16), inward.astype(jnp.bfloat16)], axis=1
+    )
+    partial = lax.dot_general(
+        back, sums, across, preferred_element_type=jnp.float32
+    ).astype(jnp.bfloat16)
+    summed = scatter_sum(partial, 2 * count, width)
+    return summed[:count], summed[count:], down_grad
+
+
+def cube_fits(mesh, tokens):
+    shape = (mesh.shape["dp"], mesh.shape["expert"])
+    rows, width = tokens.shape[0] // shape[1], tokens.shape[1] // shape[0]
+    return shape == (8, 4) and width % 128 == 0 and rows % 24 == 0 and rows <= 128
+
+
 def solution(mesh):
+    def program(tokens, *rest):
+        body = per_device_cube if cube_fits(mesh, tokens) else per_device
+        return on_mesh(mesh, body)(tokens, *rest)
+
+    return program
+
+
+def on_mesh(mesh, body):
     return jax.shard_map(
-        per_device,
+        body,
         mesh=mesh,
         in_specs=(
             P("expert", "dp"),

time: 307 us -> 129 us (0.42)
  waiting for transfers between devices: 203 us -> 0 us
  Pallas kernels: 0 us -> 67.2 us
  blocking collectives: 18.9 us -> 0 us
  between operations: 14 us -> 0.95 us
  starting transfers between devices: 6.91 us -> 0 us
  other arithmetic: 6.57 us -> 2.07 us
    reduce_scatter x1 -> x0, waiting for transfers between devices: 128 us -> none  [per_device(): lax.psum_scatter(jnp.concatenate([lax.dot_general(down_mat, hidden, acros...]
    all_gather x2 -> x0, waiting for transfers between devices: 70.2 us -> none  [the longest x1 39 us: per_device(): lax.all_gather(part_rows, 'dp', axis=2, tiled=True)]
    pallas_call x0 -> x2, Pallas kernels: none -> 67.2 us  [the longest x1 35.8 us: gather_all(): pl.pallas_call(gather_kernel, out_shape=(jax.ShapeDtypeStruct((4 * rows,...]
    all_to_all x2 -> x0, blocking collectives: 18.9 us -> none  [the longest x1 10 us: per_device(): lax.all_to_all(send_rows, 'expert', split_axis=0, concat_axis=0, tiled=True)]
    all_to_all x2 -> x0, starting transfers between devices: 6.79 us -> none  [the longest x1 3.4 us: per_device(): lax.all_to_all(expert_out, 'expert', split_axis=0, concat_axis=0, tiled=T...]
    all_to_all x2 -> x0, waiting for transfers between devices: 4.97 us -> none  [the longest x1 4.97 us: per_device(): lax.all_to_all(expert_out, 'expert', split_axis=0, concat_axis=0, tiled=T...]
    reshape x8 -> x4, local copies, waits for them, and re-layouts: 5.26 us -> 1.85 us  [the longest x2 0.93 us: joined(): lower = jnp.concatenate([none, second], axis=2).reshape(row_count, -1)]
    dot_general x11 -> x10, matrix products: 50.4 us -> 53.1 us  [the longest x1 9.61 us: per_device_cube(): lax.dot_general(rows_in, up_mat, dims, preferred_element_type=jnp.float32)]
  transfers between devices with their start and end apart: 5 -> 0, of which waited for: 4 -> 0; matrix products, arithmetic and copies ran while one was open for 9% -> 0% of each run, Pallas kernels for 0% -> 0%
where the time goes in v1:
time: 129 us
  Pallas kernels  67.2 us (52%)
  matrix products  53.1 us (41%)
  local copies, waits for them, and re-layouts  5.71 us (4%)
  other arithmetic  2.07 us (2%)
    pallas_call x1, Pallas kernels, gather_all(): pl.pallas_call(gather_kernel, out_shape=(jax.ShapeDtypeStruct((4 * rows,...  35.8 us
    pallas_call x1, Pallas kernels, scatter_sum(): pl.pallas_call(scatter_kernel, out_shape=jax.ShapeDtypeStruct((rows, widt...  31.5 us
    dot_general x1, matrix products, per_device_cube(): lax.dot_general(rows_in, up_mat, dims, preferred_element_type=jnp.float32)  9.61 us
    dot_general x1, matrix products, per_device_cube(): lax.dot_general(rows_in, gate_mat, dims, preferred_element_type=jnp.float32)  9.57 us
    dot_general x1, matrix products, per_device_cube(): lax.dot_general(up_mat, up_grad, across, preferred_element_type=jnp.float32)  6.75 us
    dot_general x1, matrix products, per_device_cube(): lax.dot_general(hidden, grads_in, (((0,), (0,)), ((), ())), preferred_ele...  6.63 us
    dot_general x1, matrix products, per_device_cube(): jnp.dot(into, everything, preferred_element_type=jnp.float32)  6.26 us
    dot_general x1, matrix products, per_device_cube(): lax.dot_general(grads_in, down_mat, dims, preferred_element_type=jnp.floa...  5.79 us

profile of v1, /device:TPU:0, one launch (start us, length us, event | category | flops | bytes accessed | tf_op | source)
XLA Modules:
  0.0 129.1 jit_solution(14509320060949000699)
XLA Ops:
  0.7 0.7 convert_bitcast_fusion.1
  1.4 0.9 pad_maximum_fusion.mine
  2.3 35.8 %shard_map.94 = (bf16[384,6144]{1,0:T(8,128)(2,1)S(1)}, bf16[4,16,128]{2,1,0:T(8,128)(2,1)S(1)}) custom-call(bf16[96,768]{1,0:T(8,128)(2,1)S(1)} %pad_maximum_fusion.mine, bf16[16,128]{1,0:T(8,128)(2,1)S(1)} %fusion.51.meta), custom_call_target="tpu_custom_call" | custom-call | tf_op jit(solution)/shard_map/pallas_call | solution.py:271
  38.1 0.0 copy-start
  38.1 2.2 %copy-done = bf16[384,6144]{1,0:T(8,128)(2,1)} copy-done((bf16[384,6144]{1,0:T(8,128)(2,1)}, bf16[384,6144]{1,0:T(8,128)(2,1)S(1)}, u32[]{:S(2)}) %copy-start) | copy-done | bytes 4718616
  40.3 0.6 gather_fusion
  40.8 0.1 fusion.53
  41.0 0.1 fusion.34
  41.1 0.2 select_convert_fusion
  41.2 0.1 fusion.44
  41.3 0.2 fusion.62
  41.6 0.8 reshape.52
  42.3 0.1 reshape.53
  42.5 0.2 fusion.61
  42.7 0.8 reshape.51
  43.5 0.1 reshape.54
  43.6 0.0 slice-start
  43.6 0.0 slice-start.1
  43.7 6.3 %convolution_convert_fusion.1 = bf16[288,6144]{1,0:T(8,128)(2,1)} fusion(bf16[384,6144]{1,0:T(8,128)(2,1)} %copy-done, bf16[144,384]{1,0:T(8,128)(2,1)S(1)} %reshape.54, bf16[144,384]{1,0:T(8,128)(2,1)S(1)} %reshape.53), kind=kOutput, calls=%fused_computation.15 | convolution fusion | flops 1361166336 | bytes 8478720 | tf_op jit(solution)/shard_map/dot_general | solution.py:342
  49.9 0.0 slice-start.2
  49.9 9.6 %fusion.10 = f32[144,1024]{1,0:T(8,128)S(1)} fusion(bf16[1,1024,6144]{2,1,0:T(8,128)(2,1)} %param.10, bf16[288,6144]{1,0:T(8,128)(2,1)} %convolution_convert_fusion.1), kind=kOutput, calls=%fused_computation.11 | convolution fusion | flops 1811939328 | bytes 14942208 | tf_op jit(solution)/shard_map/dot_general | solution.py:346
  59.5 0.0 slice-done
  59.5 0.0 slice-done.1
  59.5 0.0 slice-done.2
  59.5 5.8 %fusion = f32[144,1024]{1,0:T(8,128)S(1)} fusion(bf16[1,1024,6144]{2,1,0:T(8,128)(2,1)S(1)} %bitcast.43, bf16[288,6144]{1,0:T(8,128)(2,1)} %convolution_convert_fusion.1), kind=kOutput, calls=%fused_computation.1 | convolution fusion | flops 1811939328 | bytes 14942208 | tf_op jit(solution)/shard_map/dot_general | solution.py:351
  65.3 9.6 %multiply_convert_fusion.2 = (bf16[144,1024]{1,0:T(8,128)(2,1)S(1)}, f32[144,1024]{1,0:T(8,128)S(1)}) fusion(f32[144,1024]{1,0:T(8,128)S(1)} %fusion.10, bf16[1,1024,6144]{2,1,0:T(8,128)(2,1)} %param.11, bf16[288,6144]{1,0:T(8,128)(2,1)} %convolution_convert_fusion.1), kind=kOutput, calls=%fused_computation.32 | convolution fusion | flops 1812824064 | bytes 15826944 | tf_op jit(solution)/shard_map/dot_general | solution.py:347
  74.9 0.0 slice-start.3
  75.0 0.0 slice-start.4
  75.0 3.2 %fusion.21 = bf16[6144,144]{0,1:T(8,128)(2,1)} fusion(bf16[144,1024]{1,0:T(8,128)(2,1)S(1)} %get-tuple-element.15, bf16[1,1024,6144]{2,1,0:T(8,128)(2,1)S(1)} %bitcast.43), kind=kOutput, calls=%fused_computation.19 | convolution fusion | flops 1812824064 | bytes 14647296 | tf_op jit(solution)/shard_map/dot_general | solution.py:360
  78.2 0.0 slice-start.5
  78.2 6.8 %fusion.4 = f32[144,6144]{1,0:T(8,128)S(1)} fusion(bf16[1,1024,6144]{2,1,0:T(8,128)(2,1)} %param.11, f32[144,1024]{1,0:T(8,128)S(1)} %fusion, f32[144,1024]{1,0:T(8,128)S(1)} %fusion.10), kind=kOutput, calls=%fused_computation.5 | convolution fusion | flops 1812824064 | bytes 17301504 | tf_op jit(solution)/shard_map/dot_general | solution.py:363
  85.0 0.0 slice-done.3
  85.0 0.0 slice-done.4
  85.0 0.0 slice-done.5
  85.0 0.0 copy-start.2
  85.0 0.0 copy-start.3
  85.0 0.0 copy-start.4
  85.0 2.3 %fusion.24 = bf16[6144,144]{0,1:T(8,128)(2,1)S(1)} fusion(f32[144,6144]{1,0:T(8,128)S(1)} %fusion.4, bf16[1,1024,6144]{2,1,0:T(8,128)(2,1)S(1)} %bitcast.45, f32[144,1024]{1,0:T(8,128)S(1)} %fusion.10, f32[144,1024]{1,0:T(8,128)S(1)} %fusion, f32[144,1024]{1,0:T(8,128)S(1)} %get-tuple-element.16), kind=kOutput, calls=%fused_computation.20 | convolution fusion | flops 1815183360 | bytes 19660800 | tf_op jit(solution)/shard_map/dot_general | solution.py:361
  87.4 0.0 copy-done.2
  87.4 0.0 copy-done.3
  87.4 0.0 copy-done.4
  87.4 2.9 %convolution_convert_fusion.partial = bf16[384,6144]{1,0:T(8,128)(2,1)S(1)} fusion(bf16[6144,144]{0,1:T(8,128)(2,1)S(1)} %fusion.24, bf16[6144,144]{0,1:T(8,128)(2,1)S(1)} %copy-done.2, bf16[144,384]{1,0:T(8,128)(2,1)S(1)} %copy-done.3, bf16[144,384]{1,0:T(8,128)(2,1)S(1)} %copy-done.4), kind=kOutput, calls=%fused_computation.14 | convolution fusion | flops 1368834048 | bytes 8478720 | tf_op jit(solution)/shard_map/dot_general | solution.py:367
  90.3 0.0 copy-start.1
  90.3 31.5 %shard_map.95 = bf16[96,768]{1,0:T(8,128)(2,1)S(1)} custom-call(bf16[384,6144]{1,0:T(8,128)(2,1)S(1)} %convolution_convert_fusion.partial), custom_call_target="tpu_custom_call" | custom-call | tf_op jit(solution)/shard_map/pallas_call | solution.py:295
  121.8 0.7 fusion.60
  122.4 0.0 copy-done.1
  122.4 6.6 %convert_bitcast_fusion = bf16[1,1024,6144]{2,1,0:T(8,128)(2,1)} fusion(bf16[144,1024]{1,0:T(8,128)(2,1)S(1)} %get-tuple-element.15, bf16[288,6144]{1,0:T(8,128)(2,1)S(1)} %copy-done.1), kind=kOutput, calls=%fused_computation.13 | convolution fusion | flops 1818230784 | bytes 14647296 | tf_op jit(solution)/shard_map/dot_general | solution.py:356
  (10 shorter events, 0.1 us)
Async XLA Ops:
  38.1 2.2 %copy-start = (bf16[384,6144]{1,0:T(8,128)(2,1)}, bf16[384,6144]{1,0:T(8,128)(2,1)S(1)}, u32[]{:S(2)}) copy-start(bf16[384,6144]{1,0:T(8,128)(2,1)S(1)} %get-tuple-element.6) | copy-start | bytes 14155780
  43.6 15.9 %slice-start = ((s8[12582912]{0:T(1024)(128)(4,1)}), s8[4194304]{0:T(1024)(128)(4,1)S(1)}, s32[]{:S(2)}) async-start(s8[12582912]{0:T(1024)(128)(4,1)} %bitcast.42), calls=%async_computation | async-start | bytes 8388608
  43.6 15.9 %slice-start.1 = ((s8[12582912]{0:T(1024)(128)(4,1)}), s8[4194304]{0:T(1024)(128)(4,1)S(1)}, s32[]{:S(2)}) async-start(s8[12582912]{0:T(1024)(128)(4,1)} %bitcast.42), calls=%async_computation.1 | async-start | bytes 8388608
  49.9 9.6 %slice-start.2 = ((s8[12582912]{0:T(1024)(128)(4,1)}), s8[4194304]{0:T(1024)(128)(4,1)S(1)}, s32[]{:S(2)}) async-start(s8[12582912]{0:T(1024)(128)(4,1)} %bitcast.42), calls=%async_computation.2 | async-start | bytes 8388608
  74.9 10.0 %slice-start.3 = ((s8[12582912]{0:T(1024)(128)(4,1)}), s8[4194304]{0:T(1024)(128)(4,1)S(1)}, s32[]{:S(2)}) async-start(s8[12582912]{0:T(1024)(128)(4,1)} %bitcast.44), calls=%async_computation.3 | async-start | bytes 8388608
  75.0 10.0 %slice-start.4 = ((s8[12582912]{0:T(1024)(128)(4,1)}), s8[4194304]{0:T(1024)(128)(4,1)S(1)}, s32[]{:S(2)}) async-start(s8[12582912]{0:T(1024)(128)(4,1)} %bitcast.44), calls=%async_computation.4 | async-start | bytes 8388608
  78.2 6.8 %slice-start.5 = ((s8[12582912]{0:T(1024)(128)(4,1)}), s8[4194304]{0:T(1024)(128)(4,1)S(1)}, s32[]{:S(2)}) async-start(s8[12582912]{0:T(1024)(128)(4,1)} %bitcast.44), calls=%async_computation.5 | async-start | bytes 8388608
  85.0 2.4 %copy-start.2 = (bf16[6144,144]{0,1:T(8,128)(2,1)S(1)}, bf16[6144,144]{0,1:T(8,128)(2,1)}, u32[]{:S(2)}) copy-start(bf16[6144,144]{0,1:T(8,128)(2,1)} %fusion.21) | copy-start | bytes 5308420
  85.0 2.4 %copy-start.3 = (bf16[144,384]{1,0:T(8,128)(2,1)S(1)}, bf16[144,384]{1,0:T(8,128)(2,1)}, u32[]{:S(2)}) copy-start(bf16[144,384]{1,0:T(8,128)(2,1)} %reshape.52) | copy-start | bytes 331780
  85.0 2.4 %copy-start.4 = (bf16[144,384]{1,0:T(8,128)(2,1)S(1)}, bf16[144,384]{1,0:T(8,128)(2,1)}, u32[]{:S(2)}) copy-start(bf16[144,384]{1,0:T(8,128)(2,1)} %reshape.51) | copy-start | bytes 331780
  90.3 32.2 %copy-start.1 = (bf16[288,6144]{1,0:T(8,128)(2,1)S(1)}, bf16[288,6144]{1,0:T(8,128)(2,1)}, u32[]{:S(2)}) copy-start(bf16[288,6144]{1,0:T(8,128)(2,1)} %convolution_convert_fusion.1) | copy-start | bytes 10616836

commit v2 on v1

--- a/solution.py
+++ b/solution.py
@@ -206,11 +206,12 @@
             copy(part, step).wait_send()
 
 
-def scatter_kernel(partial, out, slots, inbox, sends, recvs):
+def scatter_kernel(partial, out, slots, kept, inbox, sends, recvs):
     rows, width = out.shape
     part_rows = rows // PARTS
     bits = own_bits()
     greet([partner(bits, name) for name in ("zh", "zl", "x", "y", "core")])
+    top = STEPS - 1
 
     def copy(part, step):
         count = 1 << step
@@ -223,41 +224,118 @@
             device_id_type=MESH,
         )
 
-    def pick(part, first, count):
-        for slot in range(first, first + count):
-            at_dp, at_expert = place(bits, flips(ORDERS[part], slot))
-            row = pl.multiple_of(at_expert * rows + part * part_rows, 16)
-            column = pl.multiple_of(at_dp * width, 128)
-            slots[part, slot] = partial[pl.ds(row, part_rows), pl.ds(column, width)]
-
-    def add(part, step, first, count):
-        for slot in range(first, first + count):
-            total = slots[part, slot].astype(jnp.float32) + inbox[
-                part, (1 << step) + slot
-            ].astype(jnp.float32)
-            slots[part, slot] = total.astype(jnp.bfloat16)
-
-    top = STEPS - 1
+    def block(part, slot):
+        at_dp, at_expert = place(bits, flips(ORDERS[part], slot))
+        row = pl.multiple_of(at_expert * rows + part * part_rows, 16)
+        column = pl.multiple_of(at_dp * width, 128)
+        return partial[pl.ds(row, part_rows), pl.ds(column, width)]
+
+    def total(part, step, slot):
+        if step == top:
+            own = block(part, slot).astype(jnp.float32)
+        else:
+            own = kept[part, slot]
+        return own + inbox[part, (1 << step) + slot].astype(jnp.float32)
+
     for part in range(PARTS):
-        pick(part, 1 << top, 1 << top)
+        for slot in range(1 << top, 2 << top):
+            slots[part, slot] = block(part, slot)
         copy(part, top).start()
-    for part in range(PARTS):
-        pick(part, 0, 1 << top)
     for step in range(top, 0, -1):
         half = 1 << (step - 1)
         for part in range(PARTS):
             copy(part, step).wait_recv()
-            add(part, step, half, half)
+            for slot in range(half, 2 * half):
+                slots[part, slot] = total(part, step, slot).astype(jnp.bfloat16)
             copy(part, step - 1).start()
         for part in range(PARTS):
-            add(part, step, 0, half)
+            for slot in range(half):
+                kept[part, slot] = total(part, step, slot)
     for part in range(PARTS):
         copy(part, 0).wait_recv()
-        total = slots[part, 0].astype(jnp.float32) + inbox[part, 1].astype(jnp.float32)
-        out[part * part_rows:(part + 1) * part_rows, :] = total.astype(jnp.bfloat16)
+        out[part * part_rows:(part + 1) * part_rows, :] = total(part, 0, 0).astype(
+            jnp.bfloat16
+        )
     for step in range(STEPS):
         for part in range(PARTS):
             copy(part, step).wait_send()
+
+
+def expert_kernel(into, back, everything, w_gate, w_up, w_down, partial, down_grad, both, sums):
+    count = into.shape[0] // 2
+    width = everything.shape[1]
+    wide = width // 8
+    step = pl.program_id(0)
+
+    @pl.when(step == 0)
+    def _():
+        @pl.loop(0, 8)
+        def _(i):
+            at = pl.ds(pl.multiple_of(i * wide, wide), wide)
+            placed = jnp.dot(into[...], everything[:, at], preferred_element_type=jnp.float32)
+            both[:, at] = placed.astype(jnp.bfloat16)
+            sums[:, at] = jnp.zeros((2 * count, wide), jnp.float32)
+
+    dims = (((1,), (1,)), ((), ()))
+    rows_in, grads_in = both[:count, :], both[count:, :]
+    pre_gate = lax.dot_general(rows_in, w_gate[0], dims, preferred_element_type=jnp.float32)
+    pre_up = lax.dot_general(rows_in, w_up[0], dims, preferred_element_type=jnp.float32)
+    hidden_grad = lax.dot_general(grads_in, w_down[0], dims, preferred_element_type=jnp.float32)
+    sigmoid_gate = jax.nn.sigmoid(pre_gate)
+    swish = pre_gate * sigmoid_gate
+    hidden = (swish * pre_up).astype(jnp.bfloat16)
+    gate_grad = (
+        hidden_grad * pre_up * sigmoid_gate * (1.0 + pre_gate * (1.0 - sigmoid_gate))
+    ).astype(jnp.bfloat16)
+    up_grad = (hidden_grad * swish).astype(jnp.bfloat16)
+    turned = hidden.T
+
+    @pl.loop(0, 8)
+    def _(i):
+        at = pl.ds(pl.multiple_of(i * wide, wide), wide)
+        sums[:count, at] += jnp.dot(hidden, w_down[0, :, at], preferred_element_type=jnp.float32)
+        sums[count:, at] += jnp.dot(
+            gate_grad, w_gate[0, :, at], preferred_element_type=jnp.float32
+        ) + jnp.dot(up_grad, w_up[0, :, at], preferred_element_type=jnp.float32)
+        down_grad[0, :, at] = jnp.dot(
+            turned, both[count:, at], preferred_element_type=jnp.float32
+        ).astype(jnp.bfloat16)
+
+    @pl.when(step == pl.num_programs(0) - 1)
+    def _():
+        @pl.loop(0, 8)
+        def _(i):
+            at = pl.ds(pl.multiple_of(i * wide, wide), wide)
+            partial[:, at] = jnp.dot(
+                back[...], sums[:, at].astype(jnp.bfloat16), preferred_element_type=jnp.float32
+            ).astype(jnp.bfloat16)
+
+
+def run_expert(into, back, everything, w_gate, w_up, w_down):
+    units, width = w_gate.shape[1:]
+    tile = 256 if units % 256 == 0 else units
+
+    def whole(array):
+        return pl.BlockSpec(array.shape, lambda i: (0, 0), pipeline_mode=pl.Buffered(1))
+
+    def tiled():
+        return pl.BlockSpec((1, tile, width), lambda i: (0, i, 0))
+
+    return pl.pallas_call(
+        expert_kernel,
+        grid=(units // tile,),
+        out_shape=(
+            jax.ShapeDtypeStruct(everything.shape, jnp.bfloat16),
+            jax.ShapeDtypeStruct(w_gate.shape, jnp.bfloat16),
+        ),
+        in_specs=[whole(into), whole(back), whole(everything), tiled(), tiled(), tiled()],
+        out_specs=(whole(everything), tiled()),
+        scratch_shapes=[
+            pltpu.VMEM((into.shape[0], width), jnp.bfloat16),
+            pltpu.VMEM((into.shape[0], width), jnp.float32),
+        ],
+        compiler_params=pltpu.CompilerParams(vmem_limit_bytes=58 << 20),
+    )(into, back, everything, w_gate, w_up, w_down)
 
 
 def vmem():
@@ -299,6 +377,7 @@
         out_specs=vmem(),
         scratch_shapes=[
             pltpu.VMEM((PARTS, 1 << STEPS, part_rows, width), jnp.bfloat16),
+            pltpu.VMEM((PARTS, 1 << (STEPS - 2), part_rows, width), jnp.float32),
             pltpu.VMEM((PARTS, 1 << STEPS, part_rows, width), jnp.bfloat16),
             dma((PARTS, STEPS)),
             dma((PARTS, STEPS)),
@@ -315,7 +394,6 @@
     count, width = tokens.shape
     capacity = 3 * count // experts
     row_count = experts * capacity
-    gate_mat, up_mat, down_mat = w_gate[0], w_up[0], w_down[0]
     meta = jnp.concatenate([routing.T, gates.T], axis=0).astype(jnp.bfloat16)
     meta = jnp.pad(meta, ((0, 12), (0, 128 - count)))
     everything, metas = gather_all(jnp.concatenate([tokens, cotangent], axis=0), meta)
@@ -339,34 +417,7 @@
         return jnp.concatenate([upper, lower], axis=0)
 
     into, back = joined(placing, weighting), joined(weighting, placing)
-    both = jnp.dot(into, everything, preferred_element_type=jnp.float32).astype(jnp.bfloat16)
-    rows_in, grads_in = both[:row_count], both[row_count:]
-    dims = (((1,), (1,)), ((), ()))
-    across = (((0,), (1,)), ((), ()))
-    pre_gate = lax.dot_general(rows_in, gate_mat, dims, preferred_element_type=jnp.float32)
-    pre_up = lax.dot_general(rows_in, up_mat, dims, preferred_element_type=jnp.float32)
-    sigmoid_gate = jax.nn.sigmoid(pre_gate)
-    swish = pre_gate * sigmoid_gate
-    hidden = (swish * pre_up).astype(jnp.bfloat16)
-    hidden_grad = lax.dot_general(grads_in, down_mat, dims, preferred_element_type=jnp.float32)
-    gate_grad = (
-        hidden_grad * pre_up * sigmoid_gate * (1.0 + pre_gate * (1.0 - sigmoid_gate))
-    ).astype(jnp.bfloat16)
-    up_grad = (hidden_grad * swish).astype(jnp.bfloat16)
-    down_grad = lax.dot_general(
-        hidden, grads_in, (((0,), (0,)), ((), ())), preferred_element_type=jnp.float32
-    )
-    down_grad = down_grad.astype(jnp.bfloat16)[None]
-    outward = lax.dot_general(down_mat, hidden, across, preferred_element_type=jnp.float32)
-    inward = lax.dot_general(
-        gate_mat, gate_grad, across, preferred_element_type=jnp.float32
-    ) + lax.dot_general(up_mat, up_grad, across, preferred_element_type=jnp.float32)
-    sums = jnp.concatenate(
-        [outward.astype(jnp.bfloat16), inward.astype(jnp.bfloat16)], axis=1
-    )
-    partial = lax.dot_general(
-        back, sums, across, preferred_element_type=jnp.float32
-    ).astype(jnp.bfloat16)
+    partial, down_grad = run_expert(into, back.T, everything, w_gate, w_up, w_down)
     summed = scatter_sum(partial, 2 * count, width)
     return summed[:count], summed[count:], down_grad
 

time: 129 us -> 123 us (0.953)
  matrix products: 53.1 us -> 0.07 us
  Pallas kernels: 67.2 us -> 112 us
  other arithmetic: 2.07 us -> 3.65 us
    dot_general x9 -> x0, matrix products: 53 us -> none  [the longest x1 9.61 us: per_device_cube(): lax.dot_general(rows_in, up_mat, dims, preferred_element_type=jnp.float32)]
    pallas_call x0 -> x1, Pallas kernels: none -> 44.7 us  [run_expert(): pl.pallas_call(expert_kernel, grid=(units // tile,), out_shape=(jax.Shape...]
    unnamed x22 -> x4, local copies, waits for them, and re-layouts: 2.23 us -> 4.45 us
where the time goes in v2:
time: 123 us; the launch traced here: 122 us
  Pallas kernels  112 us (91%)
  local copies, waits for them, and re-layouts  5.97 us (5%)
  other arithmetic  3.65 us (3%)
    pallas_call x1, Pallas kernels, run_expert(): pl.pallas_call(expert_kernel, grid=(units // tile,), out_shape=(jax.Shape...  44.7 us
    pallas_call x1, Pallas kernels, gather_all(): pl.pallas_call(gather_kernel, out_shape=(jax.ShapeDtypeStruct((4 * rows,...  35.8 us
    pallas_call x1, Pallas kernels, scatter_sum(): pl.pallas_call(scatter_kernel, out_shape=jax.ShapeDtypeStruct((rows, widt...  31.4 us
    unnamed x4, local copies, waits for them, and re-layouts  4.45 us

profile of v2, /device:TPU:0, one launch (start us, length us, event | category | flops | bytes accessed | tf_op | source)
XLA Modules:
  0.0 122.3 jit_solution(13994475692832156880)
XLA Ops:
  0.7 0.7 convert_bitcast_fusion
  1.4 0.9 pad_maximum_fusion.1.mine
  2.3 35.8 %shard_map.94 = (bf16[384,6144]{1,0:T(8,128)(2,1)S(1)}, bf16[4,16,128]{2,1,0:T(8,128)(2,1)S(1)}) custom-call(bf16[96,768]{1,0:T(8,128)(2,1)S(1)} %pad_maximum_fusion.1.mine, bf16[16,128]{1,0:T(8,128)(2,1)S(1)} %fusion.8.meta), custom_call_target="tpu_custom_call" | custom-call | tf_op jit(solution)/shard_map/pallas_call | solution.py:349
  38.1 0.0 copy-start
  38.1 2.1 %copy-done = bf16[384,6144]{1,0:T(8,128)(2,1)} copy-done((bf16[384,6144]{1,0:T(8,128)(2,1)}, bf16[384,6144]{1,0:T(8,128)(2,1)S(1)}, u32[]{:S(2)}) %copy-start) | copy-done | bytes 4718616
  40.2 0.6 gather_fusion
  40.8 0.1 fusion.10
  40.9 0.1 fusion
  41.0 0.2 select_convert_fusion
  41.2 0.1 fusion.2
  41.4 0.1 copy.12
  41.5 0.8 maximum_bitcast_fusion.back
  42.3 0.1 copy.13
  42.5 0.7 pad_maximum_fusion.into
  43.2 44.7 %shard_map.95 = (bf16[384,6144]{1,0:T(8,128)(2,1)}, bf16[1,1024,6144]{2,1,0:T(8,128)(2,1)}) custom-call(bf16[288,384]{1,0:T(8,128)(2,1)} %pad_maximum_fusion.into, bf16[384,288]{1,0:T(8,128)(2,1)} %maximum_bitcast_fusion.back, bf16[384,6144]{1,0:T(8,128)(2,1)} %copy-done, bf16[1,1024,6144]{2,1,0:T(8,128)(2,1)} %w_gate.1, bf16[1,1024,6144]{2,1,0:T(8,128)(2,1)} %w_up.1, ...), custom_call_target="tpu_custom_call" | custom-call | tf_op jit(solution)/shard_map/pallas_call | solution.py:324
  87.9 0.0 copy-start.1
  87.9 2.3 %copy-done.1 = bf16[384,6144]{1,0:T(8,128)(2,1)S(1)} copy-done((bf16[384,6144]{1,0:T(8,128)(2,1)S(1)}, bf16[384,6144]{1,0:T(8,128)(2,1)}, u32[]{:S(2)}) %copy-start.1) | copy-done | bytes 4718616
  90.2 31.4 %shard_map.96 = bf16[96,768]{1,0:T(8,128)(2,1)S(1)} custom-call(bf16[384,6144]{1,0:T(8,128)(2,1)S(1)} %copy-done.1), custom_call_target="tpu_custom_call" | custom-call | tf_op jit(solution)/shard_map/pallas_call | solution.py:373
  121.6 0.7 fusion.13
  (10 shorter events, 0.1 us)
Async XLA Ops:
  38.1 2.1 %copy-start = (bf16[384,6144]{1,0:T(8,128)(2,1)}, bf16[384,6144]{1,0:T(8,128)(2,1)S(1)}, u32[]{:S(2)}) copy-start(bf16[384,6144]{1,0:T(8,128)(2,1)S(1)} %get-tuple-element.8.everything) | copy-start | bytes 14155780
  87.9 2.3 %copy-start.1 = (bf16[384,6144]{1,0:T(8,128)(2,1)S(1)}, bf16[384,6144]{1,0:T(8,128)(2,1)}, u32[]{:S(2)}) copy-start(bf16[384,6144]{1,0:T(8,128)(2,1)} %get-tuple-element.9.partial) | copy-start | bytes 14155780

commit v3 on v2

--- a/solution.py
+++ b/solution.py
@@ -264,12 +264,12 @@
 def expert_kernel(into, back, everything, w_gate, w_up, w_down, partial, down_grad, both, sums):
     count = into.shape[0] // 2
     width = everything.shape[1]
-    wide = width // 8
+    wide = width // 4
     step = pl.program_id(0)
 
     @pl.when(step == 0)
     def _():
-        @pl.loop(0, 8)
+        @pl.loop(0, 4)
         def _(i):
             at = pl.ds(pl.multiple_of(i * wide, wide), wide)
             placed = jnp.dot(into[...], everything[:, at], preferred_element_type=jnp.float32)
@@ -278,19 +278,19 @@
 
     dims = (((1,), (1,)), ((), ()))
     rows_in, grads_in = both[:count, :], both[count:, :]
-    pre_gate = lax.dot_general(rows_in, w_gate[0], dims, preferred_element_type=jnp.float32)
-    pre_up = lax.dot_general(rows_in, w_up[0], dims, preferred_element_type=jnp.float32)
-    hidden_grad = lax.dot_general(grads_in, w_down[0], dims, preferred_element_type=jnp.float32)
+    pre_gate = lax.dot_general(w_gate[0], rows_in, dims, preferred_element_type=jnp.float32)
+    pre_up = lax.dot_general(w_up[0], rows_in, dims, preferred_element_type=jnp.float32)
+    hidden_grad = lax.dot_general(w_down[0], grads_in, dims, preferred_element_type=jnp.float32)
     sigmoid_gate = jax.nn.sigmoid(pre_gate)
     swish = pre_gate * sigmoid_gate
-    hidden = (swish * pre_up).astype(jnp.bfloat16)
+    turned = (swish * pre_up).astype(jnp.bfloat16)
     gate_grad = (
         hidden_grad * pre_up * sigmoid_gate * (1.0 + pre_gate * (1.0 - sigmoid_gate))
-    ).astype(jnp.bfloat16)
-    up_grad = (hidden_grad * swish).astype(jnp.bfloat16)
-    turned = hidden.T
-
-    @pl.loop(0, 8)
+    ).astype(jnp.bfloat16).T
+    up_grad = (hidden_grad * swish).astype(jnp.bfloat16).T
+    hidden = turned.T
+
+    @pl.loop(0, 4)
     def _(i):
         at = pl.ds(pl.multiple_of(i * wide, wide), wide)
         sums[:count, at] += jnp.dot(hidden, w_down[0, :, at], preferred_element_type=jnp.float32)
@@ -303,7 +303,7 @@
 
     @pl.when(step == pl.num_programs(0) - 1)
     def _():
-        @pl.loop(0, 8)
+        @pl.loop(0, 4)
         def _(i):
             at = pl.ds(pl.multiple_of(i * wide, wide), wide)
             partial[:, at] = jnp.dot(

time: 123 us -> 116 us (0.943)
  Pallas kernels: 112 us -> 105 us
    pallas_call x1, Pallas kernels: 44.7 us -> 38.2 us  [run_expert(): pl.pallas_call(expert_kernel, grid=(units // tile,), out_shape=(jax.Shape...]
where the time goes in v3:
time: 116 us
  Pallas kernels  105 us (91%)
  local copies, waits for them, and re-layouts  5.97 us (5%)
  other arithmetic  3.65 us (3%)
    pallas_call x1, Pallas kernels, run_expert(): pl.pallas_call(expert_kernel, grid=(units // tile,), out_shape=(jax.Shape...  38.2 us
    pallas_call x1, Pallas kernels, gather_all(): pl.pallas_call(gather_kernel, out_shape=(jax.ShapeDtypeStruct((4 * rows,...  35.8 us
    pallas_call x1, Pallas kernels, scatter_sum(): pl.pallas_call(scatter_kernel, out_shape=jax.ShapeDtypeStruct((rows, widt...  31.4 us
    unnamed x4, local copies, waits for them, and re-layouts  4.45 us

profile of v3, /device:TPU:0, one launch (start us, length us, event | category | flops | bytes accessed | tf_op | source)
XLA Modules:
  0.0 115.8 jit_solution(12958101909151209851)
XLA Ops:
  0.7 0.7 convert_bitcast_fusion
  1.4 0.9 pad_maximum_fusion.1.mine
  2.3 35.8 %shard_map.94 = (bf16[384,6144]{1,0:T(8,128)(2,1)S(1)}, bf16[4,16,128]{2,1,0:T(8,128)(2,1)S(1)}) custom-call(bf16[96,768]{1,0:T(8,128)(2,1)S(1)} %pad_maximum_fusion.1.mine, bf16[16,128]{1,0:T(8,128)(2,1)S(1)} %fusion.8.meta), custom_call_target="tpu_custom_call" | custom-call | tf_op jit(solution)/shard_map/pallas_call | solution.py:349
  38.1 0.0 copy-start
  38.1 2.1 %copy-done = bf16[384,6144]{1,0:T(8,128)(2,1)} copy-done((bf16[384,6144]{1,0:T(8,128)(2,1)}, bf16[384,6144]{1,0:T(8,128)(2,1)S(1)}, u32[]{:S(2)}) %copy-start) | copy-done | bytes 4718616
  40.2 0.6 gather_fusion
  40.8 0.1 fusion.10
  40.9 0.1 fusion
  41.0 0.2 select_convert_fusion
  41.2 0.1 fusion.2
  41.4 0.1 copy.12
  41.5 0.8 maximum_bitcast_fusion.back
  42.3 0.1 copy.13
  42.5 0.7 pad_maximum_fusion.into
  43.2 38.2 %shard_map.95 = (bf16[384,6144]{1,0:T(8,128)(2,1)}, bf16[1,1024,6144]{2,1,0:T(8,128)(2,1)}) custom-call(bf16[288,384]{1,0:T(8,128)(2,1)} %pad_maximum_fusion.into, bf16[384,288]{1,0:T(8,128)(2,1)} %maximum_bitcast_fusion.back, bf16[384,6144]{1,0:T(8,128)(2,1)} %copy-done, bf16[1,1024,6144]{2,1,0:T(8,128)(2,1)} %w_gate.1, bf16[1,1024,6144]{2,1,0:T(8,128)(2,1)} %w_up.1, ...), custom_call_target="tpu_custom_call" | custom-call | tf_op jit(solution)/shard_map/pallas_call | solution.py:324
  81.4 0.0 copy-start.1
  81.4 2.3 %copy-done.1 = bf16[384,6144]{1,0:T(8,128)(2,1)S(1)} copy-done((bf16[384,6144]{1,0:T(8,128)(2,1)S(1)}, bf16[384,6144]{1,0:T(8,128)(2,1)}, u32[]{:S(2)}) %copy-start.1) | copy-done | bytes 4718616
  83.7 31.4 %shard_map.96 = bf16[96,768]{1,0:T(8,128)(2,1)S(1)} custom-call(bf16[384,6144]{1,0:T(8,128)(2,1)S(1)} %copy-done.1), custom_call_target="tpu_custom_call" | custom-call | tf_op jit(solution)/shard_map/pallas_call | solution.py:373
  115.2 0.7 fusion.13
  (10 shorter events, 0.1 us)
Async XLA Ops:
  38.1 2.1 %copy-start = (bf16[384,6144]{1,0:T(8,128)(2,1)}, bf16[384,6144]{1,0:T(8,128)(2,1)S(1)}, u32[]{:S(2)}) copy-start(bf16[384,6144]{1,0:T(8,128)(2,1)S(1)} %get-tuple-element.8.everything) | copy-start | bytes 14155780
  81.4 2.3 %copy-start.1 = (bf16[384,6144]{1,0:T(8,128)(2,1)S(1)}, bf16[384,6144]{1,0:T(8,128)(2,1)}, u32[]{:S(2)}) copy-start(bf16[384,6144]{1,0:T(8,128)(2,1)} %get-tuple-element.9.partial) | copy-start | bytes 14155780
